TPU v7x, 32 devices: a whole 2x2x4 slice. The times are simulated.
32 devices in a mesh: pole: 2 (over y), prow: 1, pcol: 16 (over z, x, core).
Axes of the slice: x: 2, y: 2, z: 4, core: 2. Of those that a mesh axis runs over, the one named last changes fastest.
Arguments:
- anc_inverse: float32 [12288, 6144], P(('pole', 'prow'), 'pcol'), parts along dimension 0, may hold values from -8 to 8
- anc_factor: float32 [12288, 768], P(('pole', 'pcol')), parts along dimension 0, may hold values from -0.078125 to 0.078125
- win_factor: float32 [1536, 768], P('pole'), parts along dimension 0, may hold values from -0.375 to 0.375
- pivot_inverse: float32 [6, 256, 256], P('pole'), parts along dimension 0, may hold values from -6 to 6
- structure: int32 [3, 24], replicated, may hold values 0 or 1
Outputs:
- anc_columns: float32 [12288, 768], P(('pole', 'prow', 'pcol')), parts along dimension 0
- win_inverse: float32 [1536, 768], P('pole'), parts along dimension 0
There are 2 independent parts, one for each index of `pole`. A program takes and returns all parts, laid end to end along the dimension named above; an argument that names none is the same for every part. Nothing has to cross between parts.
All inputs are finite; a program needn't handle non-finite values.
Results may differ from a plain program's by a relative error of at most 0.0001.
Values sent between devices are 32-bit elements; how exact they have to be, the bound alone decides.
A program may use at most 128 MiB of HBM per device.

v0:
```python
import jax
import jax.numpy as jnp
from jax import lax
from jax.sharding import PartitionSpec as P

precise = lax.Precision.HIGHEST


def product(left, right):
    return jnp.dot(left, right, precision=precise, preferred_element_type=jnp.float32)


def on_device(anc_inverse, anc_factor, win_factor, pivot_inverse, structure):
    row_count = lax.axis_size("prow")
    col_count = lax.axis_size("pcol")
    row_index = lax.axis_index("prow")
    col_index = lax.axis_index("pcol")
    block_rows = anc_inverse.shape[0]
    block_cols = anc_inverse.shape[1]
    steps_total = pivot_inverse.shape[0]
    width = pivot_inverse.shape[1]
    all_cols = anc_factor.shape[1]
    block_count = structure.shape[1]
    ratio_cols = col_count // row_count
    share_rows = block_rows // col_count
    structure_cols = structure.T.astype(jnp.float32)
    global_rows = col_index * block_cols + lax.iota(jnp.int32, block_cols)
    onehot_rows = (
        (global_rows // width)[:, None] == lax.iota(jnp.int32, block_count)[None, :]
    ).astype(jnp.float32)
    kept_rows = product(onehot_rows, structure_cols)
    share_offset = col_index * share_rows
    share_global = (row_index * col_count + col_index) * share_rows + lax.iota(
        jnp.int32, share_rows
    )
    onehot_share = (
        (share_global // width)[:, None] == lax.iota(jnp.int32, block_count)[None, :]
    ).astype(jnp.float32)
    kept_share = product(onehot_share, structure_cols)
    slot_ids = lax.iota(jnp.int32, col_count)
    source_flag = (slot_ids // row_count == col_index - row_index * ratio_cols).astype(jnp.float32)
    pieces = jnp.tile(anc_factor.reshape(row_count, share_rows, all_cols), (ratio_cols, 1, 1))
    outgoing = pieces * source_flag[:, None, None]
    incoming = lax.all_to_all(outgoing, "pcol", split_axis=0, concat_axis=0, tiled=True)
    factor_share = jnp.sum(incoming, axis=0)
    column_store = {}
    share_store = {}
    window_blocks = {}
    for k in range(steps_total - 1, -1, -1):
        first_col = k * width
        factor_now = anc_factor[:, first_col : first_col + width] * kept_rows[:, k : k + 1]
        share_factor = factor_share[:, first_col : first_col + width] * kept_share[:, k : k + 1]
        finished = list(range(k + 1, steps_total))
        if finished:
            stacked = jnp.concatenate([column_store[j] for j in finished], axis=1)
            factor_win = win_factor[first_col + width :, first_col : first_col + width]

        def term_rows(start, count, factor_now=factor_now):
            return product(anc_inverse, factor_now)

        share_image = lax.psum_scatter(
            term_rows(jnp.int32(0), share_rows * lax.axis_size("pcol")),
            "pcol",
            scatter_dimension=0,
            tiled=True,
        )
        if finished:
            share_image = share_image + product(
                lax.dynamic_slice_in_dim(stacked, share_offset, share_rows, 0), factor_win
            )
        share_column = -share_image
        column_now = lax.all_gather(share_column, "pcol", axis=0, tiled=True)
        crossings = [product(share_store[j].T, share_factor) for j in finished]
        pivot_part = product(share_factor.T, share_column)
        cross_sums = []
        if finished:
            cross_total = lax.psum(jnp.stack(crossings), ("prow", "pcol"))
            cross_sums = [cross_total[position] for position in range(len(finished))]
        pivot_sum = lax.psum(pivot_part, ("prow", "pcol"))
        for position, j in enumerate(finished):
            running = cross_sums[position]
            for i in finished:
                running = running + product(
                    window_blocks[j, i],
                    win_factor[i * width : (i + 1) * width, first_col : first_col + width],
                )
            window_blocks[j, k] = -running
            window_blocks[k, j] = -running.T
        pivot_block = pivot_inverse[k] - pivot_sum
        for j in finished:
            pivot_block = pivot_block - product(
                win_factor[j * width : (j + 1) * width, first_col : first_col + width].T,
                window_blocks[j, k],
            )
        window_blocks[k, k] = pivot_block
        column_store[k] = column_now
        share_store[k] = share_column
    anc_columns = jnp.concatenate([share_store[k] for k in range(steps_total)], axis=1)
    win_inverse = jnp.concatenate(
        [
            jnp.concatenate([window_blocks[i, k] for k in range(steps_total)], axis=1)
            for i in range(steps_total)
        ],
        axis=0,
    )
    return (anc_columns, win_inverse)


def solution(mesh):
    in_specs = (
        P(("pole", "prow"), "pcol"),
        P(("pole", "pcol"), None),
        P("pole", None),
        P("pole", None, None),
        P(),
    )
    out_specs = (P(("pole", "prow", "pcol"), None), P("pole", None))
    return jax.shard_map(
        on_device, mesh=mesh, in_specs=in_specs, out_specs=out_specs, check_vma=False
    )
```

profile of v0, /device:TPU:0, one launch (start us, length us, event | category | flops | bytes accessed | tf_op | source)
XLA Modules:
  0.0 905.3 jit_solution(14524148858973868540)
XLA Ops:
  7.2 0.0 reduce-scatter.8.cloned.1.call-start
  7.2 1.0 fusion.40
  8.2 19.4 %convolution_bitcast_fusion = f32[6144,256]{0,1:T(8,128)} fusion(f32[6144,384]{1,0:T(8,128)} %param.5, f32[384,768]{1,0:T(8,128)} %param.6, f32[384]{0:T(512)S(1)} %get-tuple-element.7), kind=kOutput, calls=%fused_computation.3 | convolution fusion | flops 7247855616 | bytes 16123392 | tf_op jit(solution)/shard_map/dot_general | solution.py:10
  27.6 0.0 reduce-scatter.8.cloned.1.call-update
  27.6 0.2 reduce-scatter.6.cloned.1.call-start
  27.9 1.0 copy-done.2
  28.9 19.2 %convolution_bitcast_fusion.1 = f32[6144,256]{0,1:T(8,128)} fusion(f32[6144,384]{1,0:T(8,128)} %param.5, f32[384,768]{1,0:T(8,128)S(1)} %copy-done.2, f32[384]{0:T(512)S(1)} %get-tuple-element.8), kind=kOutput, calls=%fused_computation.4 | convolution fusion | flops 7247855616 | bytes 16123904 | tf_op jit(solution)/shard_map/dot_general | solution.py:10
  48.1 0.0 reduce-scatter.6.cloned.1.call-update
  48.1 8.4 broadcast_multiply_fusion
  56.5 7.4 all-to-all-start
  63.9 0.0 all-gather.3.cloned.1.call-start
  63.9 346.9 %reduce-scatter.8.cloned.1.call-done = f32[384,256]{0,1:T(8,128)} async-done(((f32[6144,256]{0,1:T(8,128)}), f32[384,256]{0,1:T(8,128)}) %reduce-scatter.8.cloned.1.call-update) | async-done | bytes 393232 | tf_op jit(solution)/shard_map/reduce_scatter | solution.py:61
  410.8 1.8 neg.30
  412.6 0.0 all-gather.3.cloned.1.call-update
  412.6 0.3 reduce-scatter.4.cloned.1.call-start
  412.9 19.2 %convolution_bitcast_fusion.2 = f32[6144,256]{0,1:T(8,128)} fusion(f32[6144,384]{1,0:T(8,128)} %param.5, f32[384,768]{1,0:T(8,128)S(1)} %copy-done.2, f32[384]{0:T(512)S(1)} %get-tuple-element.6), kind=kOutput, calls=%fused_computation.5 | convolution fusion | flops 7247855616 | bytes 16123904 | tf_op jit(solution)/shard_map/dot_general | solution.py:10
  432.1 0.0 reduce-scatter.4.cloned.1.call-update
  432.1 0.0 all-gather.5.cloned.1.call-start
  432.2 121.9 %reduce-scatter.6.cloned.1.call-done = f32[384,256]{0,1:T(8,128)} async-done(((f32[6144,256]{0,1:T(8,128)}), f32[384,256]{0,1:T(8,128)}) %reduce-scatter.6.cloned.1.call-update) | async-done | bytes 393232 | tf_op jit(solution)/shard_map/reduce_scatter | solution.py:61
  554.1 64.0 %all-gather.3.cloned.1.call-done = f32[6144,256]{0,1:T(8,128)} async-done(((f32[384,256]{0,1:T(8,128)}), f32[6144,256]{0,1:T(8,128)}) %all-gather.3.cloned.1.call-update) | async-done | bytes 6291472 | tf_op jit(solution)/shard_map/all_gather | solution.py:72
  618.1 2.6 fusion.1
  620.7 0.0 all-gather.5.cloned.1.call-update
  620.7 0.3 all-reduce.3.cloned.1.call-start
  621.0 84.6 %reduce-scatter.4.cloned.1.call-done = f32[384,256]{0,1:T(8,128)} async-done(((f32[6144,256]{0,1:T(8,128)}), f32[384,256]{0,1:T(8,128)}) %reduce-scatter.4.cloned.1.call-update) | async-done | bytes 393232 | tf_op jit(solution)/shard_map/reduce_scatter | solution.py:61
  705.7 64.0 %all-gather.5.cloned.1.call-done = f32[6144,256]{0,1:T(8,128)} async-done(((f32[384,256]{0,1:T(8,128)}), f32[6144,256]{0,1:T(8,128)}) %all-gather.5.cloned.1.call-update) | async-done | bytes 6291472 | tf_op jit(solution)/shard_map/all_gather | solution.py:72
  769.7 2.4 fusion
  772.1 0.0 copy-start
  772.1 0.0 all-to-all-done
  772.1 7.7 reduce_sum.9
  779.8 0.0 copy-done
  779.8 0.0 copy-start.1
  779.8 0.9 convolution_bitcast_fusion.7
  780.7 1.4 fusion.20
  782.1 1.6 fusion.21
  783.7 0.0 copy-done.1
  783.7 0.9 convolution_bitcast_fusion.6
  784.6 0.8 pad_maximum_fusion.2
  785.4 1.4 fusion.19
  786.8 1.6 fusion.11
  788.3 0.0 all-reduce.3.cloned.1.call-update
  788.4 0.0 slice-done
  788.4 0.8 copy.42
  789.2 0.0 copy-done.3
  789.2 0.1 pad_maximum_fusion
  789.3 1.4 copy.32
  790.7 93.1 %all-reduce.3.cloned.1.call-done = (f32[256,256]{1,0:T(8,128)}, f32[256,256]{1,0:T(8,128)}, f32[2,256,256]{1,2,0:T(8,128)}, f32[256,256]{0,1:T(8,128)}, f32[256,256]{1,0:T(8,128)}) async-done(((f32[256,256]{1,0:T(8,128)}, f32[256,256]{1,0:T(8,128)}, f32[2,256,256]{1,2,0:T(8,128)}, f32[256,256]{0,1:T(8,128)}, f32[256,256]{1,0:T(8,128)}), (f32[256,256]{1,0:T(8,128)}, f32[256,256]{1,0:T(8,128)}, ...) | async-done | bytes 1572880 | tf_op jit(solution)/shard_map/psum | solution.py:79
  883.8 1.1 bitcast_subtract_fusion
  884.9 1.4 fusion.7
  886.3 1.6 convolution_add_fusion.3
  887.9 0.0 copy-done.4
  888.0 1.5 fusion.6
  889.5 0.7 copy-done.5
  890.2 0.0 copy-done.10
  890.2 0.6 convolution_add_fusion.5
  890.8 0.6 fusion.5
  891.4 0.6 fusion.3
  892.0 0.8 copy.30
  892.9 1.7 fusion.4
  894.6 1.3 fusion.2
  895.9 0.1 pad_maximum_fusion.1
  895.9 0.3 copy.31
  896.2 0.6 copy-done.8
  896.8 0.1 copy-done.9
  896.9 1.6 maximum_maximum_fusion
  (15 shorter events, 0.1 us)
Async XLA Ops:
  7.2 403.7 %reduce-scatter.8.cloned.1.call-start = ((), (), s32[]{:S(2)}) async-start(), calls=%async_computation.6 | async-start | bytes 6684672 | tf_op jit(solution)/shard_map/reduce_scatter | solution.py:61
  27.6 1.3 copy-start.2
  27.6 526.5 %reduce-scatter.6.cloned.1.call-start = ((), (), s32[]{:S(2)}) async-start(), calls=%async_computation.5 | async-start | bytes 6684672 | tf_op jit(solution)/shard_map/reduce_scatter | solution.py:61
  56.5 715.6 %all-to-all-start = ((f32[16,384,768]{2,1,0:T(8,128)}), f32[16,384,768]{2,1,0:T(8,128)}, u32[]{:S(2)}, u32[]{:S(2)}) async-start(f32[16,384,768]{2,1,0:T(8,128)} %broadcast_multiply_fusion), calls=%async_computation.3 | async-start | bytes 37748736 | tf_op jit(solution)/shard_map/all_to_all | solution.py:44
  63.9 554.3 %all-gather.3.cloned.1.call-start = ((), (), s32[]{:S(2)}) async-start(), calls=%async_computation.7 | async-start | bytes 6684672 | tf_op jit(solution)/shard_map/all_gather | solution.py:72
  412.6 293.1 %reduce-scatter.4.cloned.1.call-start = ((), (), s32[]{:S(2)}) async-start(), calls=%async_computation.4 | async-start | bytes 6684672 | tf_op jit(solution)/shard_map/reduce_scatter | solution.py:61
  432.1 337.5 %all-gather.5.cloned.1.call-start = ((), (), s32[]{:S(2)}) async-start(), calls=%async_computation.8 | async-start | bytes 6684672 | tf_op jit(solution)/shard_map/all_gather | solution.py:72
  620.7 263.0 %all-reduce.3.cloned.1.call-start = ((), (), s32[]{:S(2)}) async-start(), calls=%async_computation.9 | async-start | bytes 3145728 | tf_op jit(solution)/shard_map/psum | solution.py:79
  772.1 7.7 copy-start
  779.8 3.9 copy-start.1
  785.4 3.0 slice-start
  785.4 3.8 copy-start.3
  790.7 97.3 %copy-start.4 = (f32[768,768]{1,0:T(8,128)S(1)}, f32[768,768]{1,0:T(8,128)}, u32[]{:S(2)}) copy-start(f32[768,768]{1,0:T(8,128)} %param.7) | copy-start | bytes 7077892
  790.7 97.3 %copy-start.7 = (f32[1,256,256]{1,2,0:T(8,128)S(1)}, f32[1,256,256]{1,2,0:T(8,128)}, u32[]{:S(2)}) copy-start(f32[1,256,256]{1,2,0:T(8,128)} %copy.42) | copy-start | bytes 786436
  883.8 6.5 copy-start.10
  889.5 0.7 copy-start.5
  892.9 3.0 copy-start.6
  895.9 0.9 copy-start.8
  895.9 1.0 copy-start.9
Sparse Core Ops, SparseCore 0:
  27.8 383.0 reduce-scatter.7
  415.3 138.7 reduce-scatter.5
  557.0 61.1 all-gather.2
  621.9 83.6 reduce-scatter.3
  708.7 60.9 all-gather.4
  788.5 95.2 all-reduce.2
where the time goes:
time: 906 us; the launch traced here: 905 us
  waiting for transfers between devices  775 us (86%)
  matrix products  80.8 us (9%)
  other arithmetic  21.5 us (2%)
  between operations  14.3 us (2%)
    reduce_scatter x3, waiting for transfers between devices, on_device(): lax.psum_scatter(term_rows(jnp.int32(0), share_rows * lax.axis_size('pcol...  553 us
    all_gather x2, waiting for transfers between devices, on_device(): column_now = lax.all_gather(share_column, 'pcol', axis=0, tiled=True)  128 us
    psum x1, waiting for transfers between devices, on_device(): pivot_sum = lax.psum(pivot_part, ('prow', 'pcol'))  93.1 us
    dot_general x20, matrix products, product(): jnp.dot(left, right, precision=precise, preferred_element_type=jnp.float32)  80.8 us
  transfers between devices with their start and end apart: 7, of which 6 were waited for; matrix products, arithmetic and copies ran while one was open for 6% of the time, Pallas kernels for 0%

commit v1 on v0

--- a/solution.py
+++ b/solution.py
@@ -69,7 +69,18 @@
                 lax.dynamic_slice_in_dim(stacked, share_offset, share_rows, 0), factor_win
             )
         share_column = -share_image
-        column_now = lax.all_gather(share_column, "pcol", axis=0, tiled=True)
+        ways = lax.axis_size("pcol")
+        up = [(d, (d + 1) % ways) for d in range(ways)]
+        down = [(d, (d - 1) % ways) for d in range(ways)]
+        earlier, later = ([share_column], [share_column])
+        for _ in range(ways // 2):
+            earlier.append(lax.ppermute(earlier[-1], "pcol", up))
+        for _ in range((ways - 1) // 2):
+            later.append(lax.ppermute(later[-1], "pcol", down))
+        line = jnp.concatenate([*earlier[::-1], *later[1:]], axis=0)
+        column_now = jnp.roll(
+            line, (lax.axis_index("pcol") - ways // 2) * share_column.shape[0], axis=0
+        )
         crossings = [product(share_store[j].T, share_factor) for j in finished]
         pivot_part = product(share_factor.T, share_column)
         cross_sums = []

time: 906 us -> 865 us (0.955)
  waiting for transfers between devices: 775 us -> 483 us
  starting transfers between devices: 8.28 us -> 218 us
  local copies, waits for them, and re-layouts: 5.82 us -> 22.5 us
  other arithmetic: 21.5 us -> 37.6 us
    reduce_scatter x3, waiting for transfers between devices: 553 us -> 312 us  [on_device(): lax.psum_scatter(term_rows(jnp.int32(0), share_rows * lax.axis_size('pcol...]
    ppermute x0 -> x30, starting transfers between devices: none -> 210 us  [the longest x16 166 us: on_device(): earlier.append(lax.ppermute(earlier[-1], 'pcol', up))]
    all_gather x2 -> x0, waiting for transfers between devices: 128 us -> none  [on_device(): column_now = lax.all_gather(share_column, 'pcol', axis=0, tiled=True)]
    ppermute x0 -> x30, waiting for transfers between devices: none -> 68.3 us  [the longest x16 49.6 us: on_device(): earlier.append(lax.ppermute(earlier[-1], 'pcol', up))]
    unnamed x24 -> x55, local copies, waits for them, and re-layouts: 4.68 us -> 21.2 us
    concatenate x0 -> x2, other arithmetic: none -> 14.7 us  [on_device(): jnp.roll(line, (lax.axis_index('pcol') - ways // 2) * share_column.shape[...]
    psum x1, waiting for transfers between devices: 93.1 us -> 103 us  [on_device(): pivot_sum = lax.psum(pivot_part, ('prow', 'pcol'))]
  transfers between devices with their start and end apart: 7 -> 35, of which waited for: 6 -> 20; matrix products, arithmetic and copies ran while one was open for 6% -> 12% of each run, Pallas kernels for 0% -> 0%
where the time goes in v1:
time: 865 us; the launch traced here: 858 us
  waiting for transfers between devices  483 us (56%)
  starting transfers between devices  218 us (25%)
  matrix products  82.9 us (10%)
  other arithmetic  37.6 us (4%)
  local copies, waits for them, and re-layouts  22.5 us (3%)
  between operations  14.6 us (2%)
    reduce_scatter x3, waiting for transfers between devices, on_device(): lax.psum_scatter(term_rows(jnp.int32(0), share_rows * lax.axis_size('pcol...  312 us
    ppermute x16, starting transfers between devices, on_device(): earlier.append(lax.ppermute(earlier[-1], 'pcol', up))  166 us
    psum x1, waiting for transfers between devices, on_device(): pivot_sum = lax.psum(pivot_part, ('prow', 'pcol'))  103 us
    dot_general x20, matrix products, product(): jnp.dot(left, right, precision=precise, preferred_element_type=jnp.float32)  82.9 us
    ppermute x16, waiting for transfers between devices, on_device(): earlier.append(lax.ppermute(earlier[-1], 'pcol', up))  49.6 us
    ppermute x14, starting transfers between devices, on_device(): later.append(lax.ppermute(later[-1], 'pcol', down))  44.2 us
    unnamed x55, local copies, waits for them, and re-layouts  21.2 us
    ppermute x14, waiting for transfers between devices, on_device(): later.append(lax.ppermute(later[-1], 'pcol', down))  18.6 us
  transfers between devices with their start and end apart: 35, of which 20 were waited for; matrix products, arithmetic and copies ran while one was open for 12% of the time, Pallas kernels for 0%

profile of v1, /device:TPU:0, one launch (start us, length us, event | category | flops | bytes accessed | tf_op | source)
XLA Modules:
  0.0 858.3 jit_solution(8340731472737733266)
XLA Ops:
  7.2 9.7 %broadcast_multiply_fusion = f32[16,384,768]{2,1,0:T(8,128)} fusion(f32[16]{0:T(128)S(1)} %compare_convert_fusion, f32[384,768]{1,0:T(8,128)} %param.8), kind=kLoop, calls=%fused_computation.8 | loop fusion | flops 4718592 | bytes 20054080 | tf_op jit(solution)/shard_map/mul | solution.py:43
  16.9 7.5 all-to-all-start
  24.9 19.2 %convolution_bitcast_fusion = f32[6144,256]{0,1:T(8,128)} fusion(f32[6144,384]{1,0:T(8,128)} %param.7, f32[384,768]{1,0:T(8,128)S(1)} %copy-done.1, f32[384]{0:T(512)S(1)} %get-tuple-element.8), kind=kOutput, calls=%fused_computation.9 | convolution fusion | flops 7247855616 | bytes 16123904 | tf_op jit(solution)/shard_map/dot_general | solution.py:10
  44.3 19.2 %convolution_bitcast_fusion.1 = f32[6144,256]{0,1:T(8,128)} fusion(f32[6144,384]{1,0:T(8,128)} %param.7, f32[384,768]{1,0:T(8,128)S(1)} %copy-done.1, f32[384]{0:T(512)S(1)} %get-tuple-element.9), kind=kOutput, calls=%fused_computation.10 | convolution fusion | flops 7247855616 | bytes 16123904 | tf_op jit(solution)/shard_map/dot_general | solution.py:10
  63.6 311.7 %reduce-scatter.8.cloned.1.call-done = f32[384,256]{0,1:T(8,128)} async-done(((f32[6144,256]{0,1:T(8,128)}), f32[384,256]{0,1:T(8,128)}) %reduce-scatter.8.cloned.1.call-update) | async-done | bytes 393232 | tf_op jit(solution)/shard_map/reduce_scatter | solution.py:61
  376.5 9.9 %collective-permute-done = f32[384,256]{0,1:T(8,128)S(1)} collective-permute-done((f32[384,256]{0,1:T(8,128)S(1)}, f32[384,256]{0,1:T(8,128)S(1)}, u32[]{:S(2)}, u32[]{:S(2)}) %collective-permute-start) | collective-permute-done | bytes 393248 | tf_op jit(solution)/shard_map/ppermute | solution.py:77
  386.4 4.4 collective-permute-start.8
  390.9 5.7 collective-permute-done.1
  396.5 4.4 collective-permute-start.9
  401.0 5.7 collective-permute-done.2
  406.6 12.3 %collective-permute-start.3 = (f32[384,256]{0,1:T(8,128)S(1)}, f32[384,256]{0,1:T(8,128)S(1)}, u32[]{:S(2)}, u32[]{:S(2)}) collective-permute-start(f32[384,256]{0,1:T(8,128)S(1)} %collective-permute-done.2), channel_id=1, source_target_pairs={{0,1},{1,2},{2,3},{3,4},{4,5},{5,6},{6,7},{7,8},{8,9},{9,10},{10,1... | collective-permute-start | bytes 1179656 | tf_op jit(solution)/shard_map/ppermute | solution.py:77
  419.0 2.3 collective-permute-start.10
  421.3 11.2 %collective-permute-done.3 = f32[384,256]{0,1:T(8,128)S(1)} collective-permute-done((f32[384,256]{0,1:T(8,128)S(1)}, f32[384,256]{0,1:T(8,128)S(1)}, u32[]{:S(2)}, u32[]{:S(2)}) %collective-permute-start.3) | collective-permute-done | bytes 393248 | tf_op jit(solution)/shard_map/ppermute | solution.py:77
  432.5 8.9 %collective-permute-start.4 = (f32[384,256]{0,1:T(8,128)S(1)}, f32[384,256]{0,1:T(8,128)S(1)}, u32[]{:S(2)}, u32[]{:S(2)}) collective-permute-start(f32[384,256]{0,1:T(8,128)S(1)} %collective-permute-done.3), channel_id=1, source_target_pairs={{0,1},{1,2},{2,3},{3,4},{4,5},{5,6},{6,7},{7,8},{8,9},{9,10},{10,1... | collective-permute-start | bytes 1179656 | tf_op jit(solution)/shard_map/ppermute | solution.py:77
  443.3 5.7 collective-permute-done.4
  449.0 6.2 collective-permute-start.5
  455.2 3.6 collective-permute-start.12
  458.8 4.7 collective-permute-done.5
  463.5 2.0 collective-permute-start.6
  465.4 19.2 %convolution_bitcast_fusion.2 = f32[6144,256]{0,1:T(8,128)} fusion(f32[6144,384]{1,0:T(8,128)} %param.7, f32[384,768]{1,0:T(8,128)S(1)} %copy-done.1, f32[384]{0:T(512)S(1)} %get-tuple-element.7), kind=kOutput, calls=%fused_computation.11 | convolution fusion | flops 7247855616 | bytes 16123904 | tf_op jit(solution)/shard_map/dot_general | solution.py:10
  484.7 9.9 %collective-permute-start.13 = (f32[384,256]{0,1:T(8,128)}, f32[384,256]{0,1:T(8,128)}, u32[]{:S(2)}, u32[]{:S(2)}) collective-permute-start(f32[384,256]{0,1:T(8,128)} %collective-permute-done.12), channel_id=1, source_target_pairs={{0,15},{1,0},{2,1},{3,2},{4,3},{5,4},{6,5},{7,6},{8,7},{9,8},{10,9... | collective-permute-start | bytes 1179656 | tf_op jit(solution)/shard_map/ppermute | solution.py:79
  494.6 58.4 %collective-permute-start.7 = (f32[384,256]{0,1:T(8,128)}, f32[384,256]{0,1:T(8,128)}, u32[]{:S(2)}, u32[]{:S(2)}) collective-permute-start(f32[384,256]{0,1:T(8,128)} %collective-permute-done.6), channel_id=1, source_target_pairs={{0,1},{1,2},{2,3},{3,4},{4,5},{5,6},{6,7},{7,8},{8,9},{9,10},{10,1... | collective-permute-start | bytes 1179656 | tf_op jit(solution)/shard_map/ppermute | solution.py:77
  554.7 1.8 constant_dynamic-update-slice_fusion.15
  556.5 1.8 constant_dynamic-update-slice_fusion.14
  558.3 1.9 constant_dynamic-update-slice_fusion.13
  560.1 1.8 constant_dynamic-update-slice_fusion.12
  568.4 1.9 constant_dynamic-update-slice_fusion.3
  570.2 1.8 constant_dynamic-update-slice_fusion.2
  572.1 1.8 constant_dynamic-update-slice_fusion.1
  574.6 2.1 fusion.3
  576.8 14.2 %collective-permute-start.15 = (f32[384,256]{0,1:T(8,128)S(1)}, f32[384,256]{0,1:T(8,128)S(1)}, u32[]{:S(2)}, u32[]{:S(2)}) collective-permute-start(f32[384,256]{0,1:T(8,128)S(1)} %fusion.3), channel_id=1, source_target_pairs={{0,1},{1,2},{2,3},{3,4},{4,5},{5,6},{6,7},{7,8},{8,9},{9,10},{10,1... | collective-permute-start | bytes 1179656 | tf_op jit(solution)/shard_map/ppermute | solution.py:77
  592.3 10.1 %collective-permute-start.16 = (f32[384,256]{0,1:T(8,128)S(1)}, f32[384,256]{0,1:T(8,128)S(1)}, u32[]{:S(2)}, u32[]{:S(2)}) collective-permute-start(f32[384,256]{0,1:T(8,128)S(1)} %collective-permute-done.15), channel_id=1, source_target_pairs={{0,1},{1,2},{2,3},{3,4},{4,5},{5,6},{6,7},{7,8},{8,9},{9,10},{10,1... | collective-permute-start | bytes 1179656 | tf_op jit(solution)/shard_map/ppermute | solution.py:77
  602.4 3.4 collective-permute-done.16
  605.8 18.7 %collective-permute-start.17 = (f32[384,256]{0,1:T(8,128)S(1)}, f32[384,256]{0,1:T(8,128)S(1)}, u32[]{:S(2)}, u32[]{:S(2)}) collective-permute-start(f32[384,256]{0,1:T(8,128)S(1)} %collective-permute-done.16), channel_id=1, source_target_pairs={{0,1},{1,2},{2,3},{3,4},{4,5},{5,6},{6,7},{7,8},{8,9},{9,10},{10,1... | collective-permute-start | bytes 1179656 | tf_op jit(solution)/shard_map/ppermute | solution.py:77
  625.9 15.3 %collective-permute-start.18 = (f32[384,256]{0,1:T(8,128)S(1)}, f32[384,256]{0,1:T(8,128)S(1)}, u32[]{:S(2)}, u32[]{:S(2)}) collective-permute-start(f32[384,256]{0,1:T(8,128)S(1)} %collective-permute-done.17), channel_id=1, source_target_pairs={{0,1},{1,2},{2,3},{3,4},{4,5},{5,6},{6,7},{7,8},{8,9},{9,10},{10,1... | collective-permute-start | bytes 1179656 | tf_op jit(solution)/shard_map/ppermute | solution.py:77
  642.5 9.3 %collective-permute-start.19 = (f32[384,256]{0,1:T(8,128)S(1)}, f32[384,256]{0,1:T(8,128)S(1)}, u32[]{:S(2)}, u32[]{:S(2)}) collective-permute-start(f32[384,256]{0,1:T(8,128)S(1)} %collective-permute-done.18), channel_id=1, source_target_pairs={{0,1},{1,2},{2,3},{3,4},{4,5},{5,6},{6,7},{7,8},{8,9},{9,10},{10,1... | collective-permute-start | bytes 1179656 | tf_op jit(solution)/shard_map/ppermute | solution.py:77
  651.9 3.2 collective-permute-done.25
  655.1 4.6 collective-permute-start.26
  659.7 3.4 collective-permute-start.20
  663.1 1.9 collective-permute-done.26
  665.0 4.7 collective-permute-start.27
  669.7 7.0 collective-permute-start.21
  676.7 6.5 collective-permute-done.27
  683.1 4.6 collective-permute-start.28
  688.0 8.8 %fusion.1 = f32[6144,256]{0,1:T(8,128)} fusion(s32[]{:T(128)S(6)} %select_n.37, f32[6144,256]{0,1:T(8,128)} %constant_dynamic-update-slice_fusion), kind=kLoop, calls=%fused_computation.13 | loop fusion | flops 1572864 | bytes 12582916 | tf_op jit(solution)/shard_map/jit(_roll_dynamic)/concatenate | solution.py:81
  696.8 4.4 collective-permute-start.29
  702.0 4.6 collective-permute-done.29
  706.6 5.9 fusion
  712.5 2.4 fusion.2
  714.9 7.6 reduce_sum.9
  723.5 1.4 fusion.23
  724.9 1.6 fusion.24
  729.5 1.6 fusion.15
  731.4 1.4 copy.34
  732.8 102.6 %all-reduce.3.cloned.1.call-done = (f32[256,256]{1,0:T(8,128)}, f32[256,256]{1,0:T(8,128)}, f32[2,256,256]{1,2,0:T(8,128)}, f32[256,256]{0,1:T(8,128)}, f32[256,256]{1,0:T(8,128)}) async-done(((f32[256,256]{1,0:T(8,128)}, f32[256,256]{1,0:T(8,128)}, f32[2,256,256]{1,2,0:T(8,128)}, f32[256,256]{0,1:T(8,128)}, f32[256,256]{1,0:T(8,128)}), (f32[256,256]{1,0:T(8,128)}, f32[256,256]{1,0:T(8,128)}, ...) | async-done | bytes 1572880 | tf_op jit(solution)/shard_map/psum | solution.py:90
  836.4 1.4 fusion.9
  837.9 1.9 convolution_add_fusion.3
  839.7 1.6 fusion.8
  841.4 1.6 convolution_add_fusion.5
  843.0 1.6 fusion.7
  844.6 1.6 fusion.5
  846.3 1.5 fusion.6
  847.8 1.5 fusion.4
  849.7 1.6 maximum_maximum_fusion
  (105 shorter events, 23.5 us)
Async XLA Ops:
  16.9 7.6 copy-start.11
  16.9 8.0 copy-start.1
  16.9 698.0 %all-to-all-start = ((f32[16,384,768]{2,1,0:T(8,128)}), f32[16,384,768]{2,1,0:T(8,128)}, u32[]{:S(2)}, u32[]{:S(2)}) async-start(f32[16,384,768]{2,1,0:T(8,128)} %broadcast_multiply_fusion), calls=%async_computation.3 | async-start | bytes 37748736 | tf_op jit(solution)/shard_map/all_to_all | solution.py:44
  24.5 350.9 %reduce-scatter.8.cloned.1.call-start = ((), (), s32[]{:S(2)}) async-start(), calls=%async_computation.6 | async-start | bytes 6684672 | tf_op jit(solution)/shard_map/reduce_scatter | solution.py:61
  44.1 530.5 %reduce-scatter.6.cloned.1.call-start = ((), (), s32[]{:S(2)}) async-start(), calls=%async_computation.5 | async-start | bytes 6684672 | tf_op jit(solution)/shard_map/reduce_scatter | solution.py:61
  63.6 648.9 %reduce-scatter.4.cloned.1.call-start = ((), (), s32[]{:S(2)}) async-start(), calls=%async_computation.4 | async-start | bytes 6684672 | tf_op jit(solution)/shard_map/reduce_scatter | solution.py:61
  376.4 10.1 %collective-permute-start = (f32[384,256]{0,1:T(8,128)S(1)}, f32[384,256]{0,1:T(8,128)S(1)}, u32[]{:S(2)}, u32[]{:S(2)}) collective-permute-start(f32[384,256]{0,1:T(8,128)S(1)} %neg.30), channel_id=1, source_target_pairs={{0,1},{1,2},{2,3},{3,4},{4,5},{5,6},{6,7},{7,8},{8,9},{9,10},{10,1... | collective-permute-start | bytes 1179656 | tf_op jit(solution)/shard_map/ppermute | solution.py:77
  386.4 10.1 %collective-permute-start.1 = (f32[384,256]{0,1:T(8,128)S(1)}, f32[384,256]{0,1:T(8,128)S(1)}, u32[]{:S(2)}, u32[]{:S(2)}) collective-permute-start(f32[384,256]{0,1:T(8,128)S(1)} %collective-permute-done), channel_id=1, source_target_pairs={{0,1},{1,2},{2,3},{3,4},{4,5},{5,6},{6,7},{7,8},{8,9},{9,10},{10,1... | collective-permute-start | bytes 1179656 | tf_op jit(solution)/shard_map/ppermute | solution.py:77
  386.4 10.1 %collective-permute-start.8 = (f32[384,256]{0,1:T(8,128)S(1)}, f32[384,256]{0,1:T(8,128)S(1)}, u32[]{:S(2)}, u32[]{:S(2)}) collective-permute-start(f32[384,256]{0,1:T(8,128)S(1)} %neg.30), channel_id=1, source_target_pairs={{0,15},{1,0},{2,1},{3,2},{4,3},{5,4},{6,5},{7,6},{8,7},{9,8},{10,9... | collective-permute-start | bytes 1179656 | tf_op jit(solution)/shard_map/ppermute | solution.py:79
  396.5 10.1 %collective-permute-start.2 = (f32[384,256]{0,1:T(8,128)S(1)}, f32[384,256]{0,1:T(8,128)S(1)}, u32[]{:S(2)}, u32[]{:S(2)}) collective-permute-start(f32[384,256]{0,1:T(8,128)S(1)} %collective-permute-done.1), channel_id=1, source_target_pairs={{0,1},{1,2},{2,3},{3,4},{4,5},{5,6},{6,7},{7,8},{8,9},{9,10},{10,1... | collective-permute-start | bytes 1179656 | tf_op jit(solution)/shard_map/ppermute | solution.py:77
  396.5 22.4 %collective-permute-start.9 = (f32[384,256]{0,1:T(8,128)S(1)}, f32[384,256]{0,1:T(8,128)S(1)}, u32[]{:S(2)}, u32[]{:S(2)}) collective-permute-start(f32[384,256]{0,1:T(8,128)S(1)} %collective-permute-done.8), channel_id=1, source_target_pairs={{0,15},{1,0},{2,1},{3,2},{4,3},{5,4},{6,5},{7,6},{8,7},{9,8},{10,9... | collective-permute-start | bytes 1179656 | tf_op jit(solution)/shard_map/ppermute | solution.py:79
  406.6 78.0 %copy-start.3 = (f32[384,256]{0,1:T(8,128)}, f32[384,256]{0,1:T(8,128)S(1)}, u32[]{:S(2)}) copy-start(f32[384,256]{0,1:T(8,128)S(1)} %collective-permute-done.2) | copy-start | bytes 1179652
  406.6 25.9 %collective-permute-start.3 = (f32[384,256]{0,1:T(8,128)S(1)}, f32[384,256]{0,1:T(8,128)S(1)}, u32[]{:S(2)}, u32[]{:S(2)}) collective-permute-start(f32[384,256]{0,1:T(8,128)S(1)} %collective-permute-done.2), channel_id=1, source_target_pairs={{0,1},{1,2},{2,3},{3,4},{4,5},{5,6},{6,7},{7,8},{8,9},{9,10},{10,1... | collective-permute-start | bytes 1179656 | tf_op jit(solution)/shard_map/ppermute | solution.py:77
  419.0 22.4 %collective-permute-start.10 = (f32[384,256]{0,1:T(8,128)S(1)}, f32[384,256]{0,1:T(8,128)S(1)}, u32[]{:S(2)}, u32[]{:S(2)}) collective-permute-start(f32[384,256]{0,1:T(8,128)S(1)} %collective-permute-done.9), channel_id=1, source_target_pairs={{0,15},{1,0},{2,1},{3,2},{4,3},{5,4},{6,5},{7,6},{8,7},{9,8},{10,9... | collective-permute-start | bytes 1179656 | tf_op jit(solution)/shard_map/ppermute | solution.py:79
  432.5 22.7 %copy-start.7 = (f32[384,256]{0,1:T(8,128)}, f32[384,256]{0,1:T(8,128)S(1)}, u32[]{:S(2)}) copy-start(f32[384,256]{0,1:T(8,128)S(1)} %collective-permute-done.3) | copy-start | bytes 1179652
  432.5 16.5 %collective-permute-start.4 = (f32[384,256]{0,1:T(8,128)S(1)}, f32[384,256]{0,1:T(8,128)S(1)}, u32[]{:S(2)}, u32[]{:S(2)}) collective-permute-start(f32[384,256]{0,1:T(8,128)S(1)} %collective-permute-done.3), channel_id=1, source_target_pairs={{0,1},{1,2},{2,3},{3,4},{4,5},{5,6},{6,7},{7,8},{8,9},{9,10},{10,1... | collective-permute-start | bytes 1179656 | tf_op jit(solution)/shard_map/ppermute | solution.py:77
  441.4 0.7 copy-start.5
  442.1 13.1 %collective-permute-start.11 = (f32[384,256]{0,1:T(8,128)S(1)}, f32[384,256]{0,1:T(8,128)}, u32[]{:S(2)}, u32[]{:S(2)}) collective-permute-start(f32[384,256]{0,1:T(8,128)S(1)} %collective-permute-done.10), channel_id=1, source_target_pairs={{0,15},{1,0},{2,1},{3,2},{4,3},{5,4},{6,5},{7,6},{8,7},{9,8},{10,9... | collective-permute-start | bytes 1179656 | tf_op jit(solution)/shard_map/ppermute | solution.py:79
  449.0 9.7 %copy-start.9 = (f32[384,256]{0,1:T(8,128)}, f32[384,256]{0,1:T(8,128)S(1)}, u32[]{:S(2)}) copy-start(f32[384,256]{0,1:T(8,128)S(1)} %collective-permute-done.4) | copy-start | bytes 1179652
  449.0 14.4 %collective-permute-start.5 = (f32[384,256]{0,1:T(8,128)S(1)}, f32[384,256]{0,1:T(8,128)}, u32[]{:S(2)}, u32[]{:S(2)}) collective-permute-start(f32[384,256]{0,1:T(8,128)S(1)} %collective-permute-done.4), channel_id=1, source_target_pairs={{0,1},{1,2},{2,3},{3,4},{4,5},{5,6},{6,7},{7,8},{8,9},{9,10},{10,1... | collective-permute-start | bytes 1179656 | tf_op jit(solution)/shard_map/ppermute | solution.py:77
  455.2 29.5 %collective-permute-start.12 = (f32[384,256]{0,1:T(8,128)}, f32[384,256]{0,1:T(8,128)}, u32[]{:S(2)}, u32[]{:S(2)}) collective-permute-start(f32[384,256]{0,1:T(8,128)} %collective-permute-done.11), channel_id=1, source_target_pairs={{0,15},{1,0},{2,1},{3,2},{4,3},{5,4},{6,5},{7,6},{8,7},{9,8},{10,9... | collective-permute-start | bytes 1179656 | tf_op jit(solution)/shard_map/ppermute | solution.py:79
  463.5 31.1 %collective-permute-start.6 = (f32[384,256]{0,1:T(8,128)}, f32[384,256]{0,1:T(8,128)}, u32[]{:S(2)}, u32[]{:S(2)}) collective-permute-start(f32[384,256]{0,1:T(8,128)} %collective-permute-done.5), channel_id=1, source_target_pairs={{0,1},{1,2},{2,3},{3,4},{4,5},{5,6},{6,7},{7,8},{8,9},{9,10},{10,1... | collective-permute-start | bytes 1179656 | tf_op jit(solution)/shard_map/ppermute | solution.py:77
  484.6 77.3 %copy-start.8 = (f32[384,256]{0,1:T(8,128)S(1)}, f32[384,256]{0,1:T(8,128)}, u32[]{:S(2)}) copy-start(f32[384,256]{0,1:T(8,128)} %copy-done.7) | copy-start | bytes 1179652
  484.6 78.1 %copy-start.4 = (f32[384,256]{0,1:T(8,128)S(1)}, f32[384,256]{0,1:T(8,128)}, u32[]{:S(2)}) copy-start(f32[384,256]{0,1:T(8,128)} %copy-done.3) | copy-start | bytes 1179652
  484.6 80.5 %copy-start = (f32[384,256]{0,1:T(8,128)S(1)}, f32[384,256]{0,1:T(8,128)}, u32[]{:S(2)}) copy-start(f32[384,256]{0,1:T(8,128)} %reduce-scatter.8.cloned.1.call-done) | copy-start | bytes 1179652
  484.7 82.9 %copy-start.6 = (f32[384,256]{0,1:T(8,128)S(1)}, f32[384,256]{0,1:T(8,128)}, u32[]{:S(2)}) copy-start(f32[384,256]{0,1:T(8,128)} %copy-done.5) | copy-start | bytes 1179652
  484.7 350.6 %all-reduce.3.cloned.1.call-start = ((), (), s32[]{:S(2)}) async-start(), calls=%async_computation.7 | async-start | bytes 3145728 | tf_op jit(solution)/shard_map/psum | solution.py:90
  484.7 69.5 %collective-permute-start.13 = (f32[384,256]{0,1:T(8,128)}, f32[384,256]{0,1:T(8,128)}, u32[]{:S(2)}, u32[]{:S(2)}) collective-permute-start(f32[384,256]{0,1:T(8,128)} %collective-permute-done.12), channel_id=1, source_target_pairs={{0,15},{1,0},{2,1},{3,2},{4,3},{5,4},{6,5},{7,6},{8,7},{9,8},{10,9... | collective-permute-start | bytes 1179656 | tf_op jit(solution)/shard_map/ppermute | solution.py:79
  494.6 60.1 %collective-permute-start.7 = (f32[384,256]{0,1:T(8,128)}, f32[384,256]{0,1:T(8,128)}, u32[]{:S(2)}, u32[]{:S(2)}) collective-permute-start(f32[384,256]{0,1:T(8,128)} %collective-permute-done.6), channel_id=1, source_target_pairs={{0,1},{1,2},{2,3},{3,4},{4,5},{5,6},{6,7},{7,8},{8,9},{9,10},{10,1... | collective-permute-start | bytes 1179656 | tf_op jit(solution)/shard_map/ppermute | solution.py:77
  554.3 19.6 %collective-permute-start.14 = (f32[384,256]{0,1:T(8,128)}, f32[384,256]{0,1:T(8,128)S(1)}, u32[]{:S(2)}, u32[]{:S(2)}) collective-permute-start(f32[384,256]{0,1:T(8,128)} %collective-permute-done.13), channel_id=1, source_target_pairs={{0,15},{1,0},{2,1},{3,2},{4,3},{5,4},{6,5},{7,6},{8,7},{9,8},{10,9... | collective-permute-start | bytes 1179656 | tf_op jit(solution)/shard_map/ppermute | solution.py:79
  576.8 15.5 %collective-permute-start.15 = (f32[384,256]{0,1:T(8,128)S(1)}, f32[384,256]{0,1:T(8,128)S(1)}, u32[]{:S(2)}, u32[]{:S(2)}) collective-permute-start(f32[384,256]{0,1:T(8,128)S(1)} %fusion.3), channel_id=1, source_target_pairs={{0,1},{1,2},{2,3},{3,4},{4,5},{5,6},{6,7},{7,8},{8,9},{9,10},{10,1... | collective-permute-start | bytes 1179656 | tf_op jit(solution)/shard_map/ppermute | solution.py:77
  592.3 13.5 %collective-permute-start.16 = (f32[384,256]{0,1:T(8,128)S(1)}, f32[384,256]{0,1:T(8,128)S(1)}, u32[]{:S(2)}, u32[]{:S(2)}) collective-permute-start(f32[384,256]{0,1:T(8,128)S(1)} %collective-permute-done.15), channel_id=1, source_target_pairs={{0,1},{1,2},{2,3},{3,4},{4,5},{5,6},{6,7},{7,8},{8,9},{9,10},{10,1... | collective-permute-start | bytes 1179656 | tf_op jit(solution)/shard_map/ppermute | solution.py:77
  602.4 22.1 %collective-permute-start.23 = (f32[384,256]{0,1:T(8,128)S(1)}, f32[384,256]{0,1:T(8,128)S(1)}, u32[]{:S(2)}, u32[]{:S(2)}) collective-permute-start(f32[384,256]{0,1:T(8,128)S(1)} %fusion.3), channel_id=1, source_target_pairs={{0,15},{1,0},{2,1},{3,2},{4,3},{5,4},{6,5},{7,6},{8,7},{9,8},{10,9... | collective-permute-start | bytes 1179656 | tf_op jit(solution)/shard_map/ppermute | solution.py:79
  605.8 20.1 %collective-permute-start.17 = (f32[384,256]{0,1:T(8,128)S(1)}, f32[384,256]{0,1:T(8,128)S(1)}, u32[]{:S(2)}, u32[]{:S(2)}) collective-permute-start(f32[384,256]{0,1:T(8,128)S(1)} %collective-permute-done.16), channel_id=1, source_target_pairs={{0,1},{1,2},{2,3},{3,4},{4,5},{5,6},{6,7},{7,8},{8,9},{9,10},{10,1... | collective-permute-start | bytes 1179656 | tf_op jit(solution)/shard_map/ppermute | solution.py:77
  624.5 17.9 %collective-permute-start.24 = (f32[384,256]{0,1:T(8,128)S(1)}, f32[384,256]{0,1:T(8,128)S(1)}, u32[]{:S(2)}, u32[]{:S(2)}) collective-permute-start(f32[384,256]{0,1:T(8,128)S(1)} %collective-permute-done.23), channel_id=1, source_target_pairs={{0,15},{1,0},{2,1},{3,2},{4,3},{5,4},{6,5},{7,6},{8,7},{9,8},{10,9... | collective-permute-start | bytes 1179656 | tf_op jit(solution)/shard_map/ppermute | solution.py:79
  625.9 16.7 %collective-permute-start.18 = (f32[384,256]{0,1:T(8,128)S(1)}, f32[384,256]{0,1:T(8,128)S(1)}, u32[]{:S(2)}, u32[]{:S(2)}) collective-permute-start(f32[384,256]{0,1:T(8,128)S(1)} %collective-permute-done.17), channel_id=1, source_target_pairs={{0,1},{1,2},{2,3},{3,4},{4,5},{5,6},{6,7},{7,8},{8,9},{9,10},{10,1... | collective-permute-start | bytes 1179656 | tf_op jit(solution)/shard_map/ppermute | solution.py:77
  642.4 12.7 %collective-permute-start.25 = (f32[384,256]{0,1:T(8,128)S(1)}, f32[384,256]{0,1:T(8,128)S(1)}, u32[]{:S(2)}, u32[]{:S(2)}) collective-permute-start(f32[384,256]{0,1:T(8,128)S(1)} %collective-permute-done.24), channel_id=1, source_target_pairs={{0,15},{1,0},{2,1},{3,2},{4,3},{5,4},{6,5},{7,6},{8,7},{9,8},{10,9... | collective-permute-start | bytes 1179656 | tf_op jit(solution)/shard_map/ppermute | solution.py:79
  642.5 17.2 %collective-permute-start.19 = (f32[384,256]{0,1:T(8,128)S(1)}, f32[384,256]{0,1:T(8,128)S(1)}, u32[]{:S(2)}, u32[]{:S(2)}) collective-permute-start(f32[384,256]{0,1:T(8,128)S(1)} %collective-permute-done.18), channel_id=1, source_target_pairs={{0,1},{1,2},{2,3},{3,4},{4,5},{5,6},{6,7},{7,8},{8,9},{9,10},{10,1... | collective-permute-start | bytes 1179656 | tf_op jit(solution)/shard_map/ppermute | solution.py:77
  655.1 9.9 %collective-permute-start.26 = (f32[384,256]{0,1:T(8,128)S(1)}, f32[384,256]{0,1:T(8,128)S(1)}, u32[]{:S(2)}, u32[]{:S(2)}) collective-permute-start(f32[384,256]{0,1:T(8,128)S(1)} %collective-permute-done.25), channel_id=1, source_target_pairs={{0,15},{1,0},{2,1},{3,2},{4,3},{5,4},{6,5},{7,6},{8,7},{9,8},{10,9... | collective-permute-start | bytes 1179656 | tf_op jit(solution)/shard_map/ppermute | solution.py:79
  659.7 10.0 %collective-permute-start.20 = (f32[384,256]{0,1:T(8,128)S(1)}, f32[384,256]{0,1:T(8,128)S(1)}, u32[]{:S(2)}, u32[]{:S(2)}) collective-permute-start(f32[384,256]{0,1:T(8,128)S(1)} %collective-permute-done.19), channel_id=1, source_target_pairs={{0,1},{1,2},{2,3},{3,4},{4,5},{5,6},{6,7},{7,8},{8,9},{9,10},{10,1... | collective-permute-start | bytes 1179656 | tf_op jit(solution)/shard_map/ppermute | solution.py:77
  665.0 18.2 %collective-permute-start.27 = (f32[384,256]{0,1:T(8,128)S(1)}, f32[384,256]{0,1:T(8,128)S(1)}, u32[]{:S(2)}, u32[]{:S(2)}) collective-permute-start(f32[384,256]{0,1:T(8,128)S(1)} %collective-permute-done.26), channel_id=1, source_target_pairs={{0,15},{1,0},{2,1},{3,2},{4,3},{5,4},{6,5},{7,6},{8,7},{9,8},{10,9... | collective-permute-start | bytes 1179656 | tf_op jit(solution)/shard_map/ppermute | solution.py:79
  669.7 18.3 %collective-permute-start.21 = (f32[384,256]{0,1:T(8,128)S(1)}, f32[384,256]{0,1:T(8,128)S(1)}, u32[]{:S(2)}, u32[]{:S(2)}) collective-permute-start(f32[384,256]{0,1:T(8,128)S(1)} %collective-permute-done.20), channel_id=1, source_target_pairs={{0,1},{1,2},{2,3},{3,4},{4,5},{5,6},{6,7},{7,8},{8,9},{9,10},{10,1... | collective-permute-start | bytes 1179656 | tf_op jit(solution)/shard_map/ppermute | solution.py:77
  683.1 13.7 %collective-permute-start.28 = (f32[384,256]{0,1:T(8,128)S(1)}, f32[384,256]{0,1:T(8,128)S(1)}, u32[]{:S(2)}, u32[]{:S(2)}) collective-permute-start(f32[384,256]{0,1:T(8,128)S(1)} %collective-permute-done.27), channel_id=1, source_target_pairs={{0,15},{1,0},{2,1},{3,2},{4,3},{5,4},{6,5},{7,6},{8,7},{9,8},{10,9... | collective-permute-start | bytes 1179656 | tf_op jit(solution)/shard_map/ppermute | solution.py:79
  688.0 13.2 %collective-permute-start.22 = (f32[384,256]{0,1:T(8,128)S(1)}, f32[384,256]{0,1:T(8,128)S(1)}, u32[]{:S(2)}, u32[]{:S(2)}) collective-permute-start(f32[384,256]{0,1:T(8,128)S(1)} %collective-permute-done.21), channel_id=1, source_target_pairs={{0,1},{1,2},{2,3},{3,4},{4,5},{5,6},{6,7},{7,8},{8,9},{9,10},{10,1... | collective-permute-start | bytes 1179656 | tf_op jit(solution)/shard_map/ppermute | solution.py:77
  696.8 9.7 %collective-permute-start.29 = (f32[384,256]{0,1:T(8,128)S(1)}, f32[384,256]{0,1:T(8,128)S(1)}, u32[]{:S(2)}, u32[]{:S(2)}) collective-permute-start(f32[384,256]{0,1:T(8,128)S(1)} %collective-permute-done.28), channel_id=1, source_target_pairs={{0,15},{1,0},{2,1},{3,2},{4,3},{5,4},{6,5},{7,6},{8,7},{9,8},{10,9... | collective-permute-start | bytes 1179656 | tf_op jit(solution)/shard_map/ppermute | solution.py:79
  722.6 8.5 slice-start
  731.4 114.9 %copy-start.2 = (f32[3,256,256]{2,1,0:T(8,128)S(1)}, f32[3,256,256]{2,1,0:T(8,128)}, u32[]{:S(2)}) copy-start(f32[3,256,256]{2,1,0:T(8,128)} %param.10) | copy-start | bytes 2359300
  835.3 11.0 %copy-start.10 = (f32[256,256]{1,0:T(8,128)S(1)}, f32[256,256]{1,0:T(8,128)}, u32[]{:S(2)}) copy-start(f32[256,256]{1,0:T(8,128)} %get-tuple-element.14) | copy-start | bytes 786436
Sparse Core Ops, SparseCore 0:
  44.2 331.0 reduce-scatter.7
  379.8 125.9 reduce-scatter.5
  509.7 179.4 reduce-scatter.3
  731.3 104.0 all-reduce.2
